TPU v7x, 32 devices: a whole 2x2x4 slice. The times are simulated.
32 devices in a mesh: scen: 2 (over x), tile: 16 (over z, y, core).
Axes of the slice: x: 2, y: 2, z: 4, core: 2. Of those that a mesh axis runs over, the one named last changes fastest.
Arguments:
- regional: float32 [4096, 768], P(('scen', 'tile')), parts along dimension 0, may hold values from -6 to 6
- row_weight: float32 [4096, 1], P(('scen', 'tile')), parts along dimension 0, may hold values from 0.25 to 1.75
- row_seg: int32 [4096, 1], P(('scen', 'tile')), parts along dimension 0, may hold values from 0 to 15; in each aligned block of 128 rows (0 to 127, 128 to 255, ...) at most 16 rows name the same one
- row_col: int32 [4096, 1], P(('scen', 'tile')), parts along dimension 0, may hold values from 0 to 63
- box_owner: int32 [8], P('scen'), parts along dimension 0, may hold values from 0 to 3, as said below
- cell_class: int32 [512, 128, 128], P(('scen', 'tile')), parts along dimension 0, may hold values from 0 to 31
- soil_props: float32 [3, 16], replicated, may hold values from 0.5 to 2
- build_props: float32 [16, 3, 16], replicated, may hold values from 0.5 to 2
- real_ids: int32 [2], P('scen'), parts along dimension 0, may hold values from 0 to 15
- disp_prev: float32 [512, 1, 3, 128, 128], P(('scen', 'tile')), parts along dimension 0, may hold values from -6 to 6
- disp_now: float32 [512, 1, 3, 128, 128], P(('scen', 'tile')), parts along dimension 0, may hold values from -6 to 6
Outputs:
- disp_next: float32 [512, 1, 3, 128, 128], P(('scen', 'tile')), parts along dimension 0
There are 2 independent parts, one for each index of `scen`. A program takes and returns all parts, laid end to end along the dimension named above; an argument that names none is the same for every part. Nothing has to cross between parts.
Inputs may be any that keep to these rules, and one draw needn't show every extreme that they name: `row_seg`: the rows of one device name one segment at most 16 times; some device's rows name some segment exactly 16 times. `box_owner`: each owner slot holds exactly one box. `cell_class`: classes below 16 are soil, the others building.
All inputs are finite; a program needn't handle non-finite values.
Results may differ from a plain program's by a relative error of at most 0.00005.
Values sent between devices are 32-bit elements; how exact they have to be, the bound alone decides.
A program may use at most 128 MiB of HBM per device.

v0:
```python
import jax
import jax.numpy as jnp
from jax import lax
from jax.sharding import PartitionSpec as P

SPAN = 4


TIME_STEP = 0.04
HIGHEST = lax.Precision.HIGHEST


def padded(value, sides, width):
    for axis, dim in sides:
        count, length = (lax.axis_size(axis), value.shape[dim])
        up = [(i, (i + 1) % count) for i in range(count)]
        down = [(j, i) for i, j in up]
        last = lax.slice_in_dim(value, length - width, length, axis=dim)
        leading = lax.slice_in_dim(value, 0, width, axis=dim)
        before = lax.ppermute(last, axis, up)
        after = lax.ppermute(leading, axis, down)
        value = jnp.concatenate([before, value, after], axis=dim)
    return value


def window(array, trim, axis, delta):
    index = []
    for dim in range(array.ndim):
        if dim in (0, 3, 4):
            shift = delta if dim == axis else 0
            index.append(slice(trim + shift, array.shape[dim] - trim + shift))
        else:
            index.append(slice(None))
    return array[tuple(index)]


def widen(array, width):
    return jnp.pad(array, ((0, 0), (0, 0), (0, 0), (width, width), (width, width)))


def elastic(disp_ext, bulk_ext, shear_ext):
    disp = widen(disp_ext, 2)
    bulk = widen(bulk_ext, 1)
    shear = widen(shear_ext, 1)
    centre = window(disp, 2, 0, 0)
    shear_mid = window(shear, 1, 0, 0)
    diffusion = None
    for axis in (0, 3, 4):
        upper = window(disp, 2, axis, 1)
        lower = window(disp, 2, axis, -1)
        face_up = 0.5 * (shear_mid + window(shear, 1, axis, 1))
        face_down = 0.5 * (shear_mid + window(shear, 1, axis, -1))
        term = face_up * (upper - centre) - face_down * (centre - lower)
        diffusion = term if diffusion is None else diffusion + term
    spread = None
    for comp, axis in ((0, 0), (1, 3), (2, 4)):
        part = disp[:, :, comp : comp + 1]
        term = 0.5 * (window(part, 1, axis, 1) - window(part, 1, axis, -1))
        spread = term if spread is None else spread + term
    flux = bulk * spread
    pushes = []
    for axis in (0, 3, 4):
        pushes.append(0.5 * (window(flux, 1, axis, 1) - window(flux, 1, axis, -1)))
    return diffusion + jnp.concatenate(pushes, axis=2)


def clear_rims(extended, width, position):
    extent = extended.shape[0]
    indices = jnp.arange(extent, dtype=jnp.int32)
    keep = jnp.logical_and(
        jnp.logical_or(indices >= width, position > 0),
        jnp.logical_or(indices < extent - width, position < SPAN - 1),
    )
    keep = keep.reshape((extent,) + (1,) * (extended.ndim - 1))
    return jnp.where(keep, extended, jnp.zeros_like(extended))


def receive(outgoing, columns, cells_x, depth):
    incoming, sources = (
        lax.all_to_all(outgoing, "tile", split_axis=0, concat_axis=0, tiled=True),
        lax.all_to_all(columns, "tile", split_axis=0, concat_axis=0, tiled=True),
    )
    levels = incoming.shape[1] // (3 * depth)
    picks = (jnp.arange(4 * cells_x, dtype=jnp.int32)[:, None] == sources[None, :]).astype(
        jnp.float32
    )
    summed = jnp.dot(picks, incoming, precision=HIGHEST, preferred_element_type=jnp.float32)
    summed = jnp.transpose(summed.reshape(cells_x, 4, levels, 3, depth), (0, 2, 3, 1, 4))
    blank = jnp.zeros((cells_x, levels, 3, 1, depth), jnp.float32)
    return jnp.concatenate(
        [blank, summed[:, :, :, 0:2], blank, blank, blank, blank, summed[:, :, :, 2:4], blank],
        axis=3,
    )


def state_rims(state, position):
    return clear_rims(padded(state, (("tile", 0),), 2), 2, position)


def band_rims(band, position):
    return clear_rims(padded(band, (("tile", 0),), 2), 2, position)


def material(cell_class, soil_props, build_props, real_ids, position):
    ext_class = padded(cell_class, (("tile", 0),), 1)
    reals = real_ids.shape[0]
    kinds = soil_props.shape[1]
    entries = build_props.shape[0]
    pick = (real_ids[:, None] == jnp.arange(entries, dtype=jnp.int32)[None, :]).astype(jnp.float32)
    chosen = jnp.dot(
        pick,
        build_props.reshape(entries, 3 * kinds),
        precision=HIGHEST,
        preferred_element_type=jnp.float32,
    )
    soil = soil_props[None]
    table = jnp.concatenate([soil, chosen.reshape(reals, 3, kinds)], axis=2).reshape(
        reals * 3, 2 * kinds
    )
    onehot = (jnp.arange(2 * kinds, dtype=jnp.int32)[:, None] == ext_class.reshape(1, -1)).astype(
        jnp.float32
    )
    values = jnp.dot(table, onehot, precision=HIGHEST, preferred_element_type=jnp.float32)
    values = values.reshape((reals, 3) + ext_class.shape)
    return clear_rims(jnp.transpose(values, (2, 0, 1, 3, 4)), 1, position)


def shards(
    regional,
    row_weight,
    row_seg,
    row_col,
    box_owner,
    cell_class,
    soil_props,
    build_props,
    real_ids,
    disp_prev,
    disp_now,
):
    count = lax.axis_size("tile")
    place = lax.axis_index("tile")
    position = (place + count - SPAN // 2) % SPAN
    row_total = regional.shape[0]
    capacity = max(2, 2 * row_total // count)
    cells_x = disp_now.shape[0]
    across = disp_now.shape[3]
    depth = disp_now.shape[4]
    box_total = box_owner.shape[0]
    segment = row_seg[:, 0]
    box_of = segment // SPAN
    owner = jnp.sum(
        jnp.where(
            box_of[:, None] == jnp.arange(box_total, dtype=jnp.int32)[None, :],
            box_owner[None, :],
            0,
        ),
        axis=1,
    )
    target = (owner * SPAN + SPAN // 2 + segment % SPAN) % count
    chosen = (target[:, None] == jnp.arange(count, dtype=jnp.int32)[None, :]).astype(jnp.int32)
    rank = jnp.sum((jnp.cumsum(chosen, axis=0) - chosen) * chosen, axis=1)
    slot_of = target * capacity + rank
    outgoing = (
        jnp.zeros((count * capacity, regional.shape[1]), jnp.float32)
        .at[slot_of]
        .set(regional * row_weight)
    )
    columns = jnp.full((count * capacity,), -1, jnp.int32).at[slot_of].set(row_col[:, 0])
    values = material(cell_class, soil_props, build_props, real_ids, position)
    lam_mu = values[:, :, 0:1] + values[:, :, 1:2]
    shear = values[:, :, 1:2]
    inverse = values[1:-1, :, 2:3]
    bulk_slab = jnp.concatenate([lam_mu[:, :, :, 0:5], lam_mu[:, :, :, across - 5 :]], axis=3)
    shear_slab = jnp.concatenate([shear[:, :, :, 0:5], shear[:, :, :, across - 5 :]], axis=3)
    slab_rows = jnp.arange(10, dtype=jnp.int32)
    outer = (
        jnp.logical_or(slab_rows < 2, slab_rows >= 8).astype(jnp.float32).reshape(1, 1, 1, 10, 1)
    )
    inner = 1.0 - outer
    both_levels = receive(outgoing, columns, cells_x, depth)
    previous, state = (disp_prev, disp_now)
    for level in range(2):
        band = both_levels[:, level : level + 1]
        state_ext = state_rims(state, position)
        band_ext = band_rims(band, position)
        from_outer = elastic(band_ext * outer, bulk_slab, shear_slab)
        from_inner = elastic(band_ext * inner, bulk_slab, shear_slab)
        force = inner * from_outer - outer * from_inner
        rhs = elastic(state_ext, lam_mu, shear)
        rhs = jnp.concatenate(
            [
                rhs[:, :, :, 0:4] + force[:, :, :, 0:4],
                rhs[:, :, :, 4 : across - 4],
                rhs[:, :, :, across - 4 :] + force[:, :, :, 6:10],
            ],
            axis=3,
        )
        previous, state = (state, 2.0 * state - previous + TIME_STEP * inverse * rhs)
    return state


def solution(mesh):
    return jax.shard_map(
        shards,
        mesh=mesh,
        in_specs=(
            P(("scen", "tile"), None),
            P(("scen", "tile"), None),
            P(("scen", "tile"), None),
            P(("scen", "tile"), None),
            P("scen"),
            P(("scen", "tile"), None, None),
            P(),
            P(),
            P("scen"),
            P(("scen", "tile"), None, None, None, None),
            P(("scen", "tile"), None, None, None, None),
        ),
        out_specs=P(("scen", "tile"), None, None, None, None),
        check_vma=False,
    )
```

profile of v0, /device:TPU:0, one launch (start us, length us, event | category | flops | bytes accessed | tf_op | source)
XLA Modules:
  0.0 167.7 jit_solution(6827427388920931827)
XLA Ops:
  4.4 7.4 %all-to-all-start = ((s32[16,16,1]{1,2,0:T(1,128)}), s32[16,16,1]{1,2,0:T(1,128)S(1)}, u32[]{:S(2)}, u32[]{:S(2)}) async-start(s32[16,16,1]{1,2,0:T(1,128)} %bitcast.26), calls=%async_computation | async-start | bytes 16384 | tf_op jit(solution)/shard_map/all_to_all | solution.py:81
  12.7 4.4 %collective-permute-start.1 = (s32[1,128,128]{2,1,0:T(8,128)S(1)}, s32[1,128,128]{2,1,0:T(8,128)S(1)}, u32[]{:S(2)}, u32[]{:S(2)}) collective-permute-start(s32[1,128,128]{2,1,0:T(8,128)S(1)} %get-tuple-element.39), channel_id=1, source_target_pairs={{1,0},{2,1},{3,2},{4,3},{5,4},{6,5},{7,6},{8,7},{9,8},{10,9},{11,1... | collective-permute-start | bytes 196616 | tf_op jit(solution)/shard_map/ppermute | solution.py:21
  19.2 4.4 %collective-permute-start.3 = (f32[2,1,3,128,128]{4,3,2,1,0:T(8,128)}, f32[2,1,3,128,128]{4,3,2,1,0:T(8,128)}, u32[]{:S(2)}, u32[]{:S(2)}) collective-permute-start(f32[2,1,3,128,128]{4,3,2,1,0:T(8,128)} %get-tuple-element.29), channel_id=1, source_target_pairs={{1,0},{2,1},{3,2},{4,3},{5,4},{6,5},{7,6},{8,7},{9,8},{10,9},{11,1... | collective-permute-start | bytes 1179656 | tf_op jit(solution)/shard_map/ppermute | solution.py:21
  25.4 2.5 %scatter_custom_fusion.1 = f32[256,768]{1,0:T(8,128)} fusion(s32[128]{0:T(128)S(1)} %fusion.229, f32[128,768]{1,0:T(8,128)} %param.11, f32[]{:T(128)} %constant.84.clone.1, f32[128]{0:T(128)} %bitcast.98), kind=kCustom, calls=%fused_computation.250 | custom fusion | flops 98304 | bytes 1180164 | tf_op jit(solution)/shard_map/scatter | solution.py:167
  27.9 5.8 %all-to-all-start.1 = ((f32[16,16,768]{2,1,0:T(8,128)}), f32[16,16,768]{2,1,0:T(8,128)}, u32[]{:S(2)}, u32[]{:S(2)}) async-start(f32[16,16,768]{2,1,0:T(8,128)} %bitcast.30), calls=%async_computation.1 | async-start | bytes 1572864 | tf_op jit(solution)/shard_map/all_to_all | solution.py:80
  35.7 5.4 %fusion = pred[4,8,2304,128]{3,1,2,0:T(8,128)(4,1)S(1)} fusion(s32[294912]{0:T(1024)S(1)} %bitcast.92), kind=kLoop, calls=%fused_computation.3 | loop fusion | flops 9437184 | bytes 10616832
  41.2 10.7 %copy.119 = pred[4,8,2304,128]{3,2,1,0:T(32,128)(4,1)S(1)} copy(pred[4,8,2304,128]{3,1,2,0:T(8,128)(4,1)S(1)} %fusion) | data formatting | bytes 18874368
  51.8 17.3 %fusion.1 = f32[3,18,128,128]{3,0,2,1:T(4,128)S(1)} fusion(pred[18,128,128,32]{2,1,0,3:T(32,128)(4,1)S(1)} %bitcast.91, f32[1,3,16]{2,1,0:T(4,128)S(1)} %copy.110, f32[1,3,16]{2,1,0:T(4,128)S(1)} %bitcast.99), kind=kOutput, calls=%fused_computation.4 | convolution fusion | flops 339738720 | bytes 12976512 | tf_op jit(solution)/shard_map/dot_general | solution.py:123
  73.8 2.3 %maximum_select_fusion = f32[20,1,3,128,128]{4,3,2,1,0:T(8,128)S(1)} fusion(f32[2,1,3,128,128]{4,3,2,1,0:T(8,128)} %collective-permute-done.3, f32[16,1,3,128,128]{4,3,2,1,0:T(8,128)S(1)} %copy-done, f32[2,1,3,128,128]{4,3,2,1,0:T(8,128)} %collective-permute-done.2, pred[20]{0:T(512)(128)(4,1)S(1)} %or_and_fusion), kind=kLoop, calls=%fused_computation.30 | loop fusion | flops 2949120 | bytes 7864340 | tf_op jit(solution)/shard_map/jit(_where)/select_n | solution.py:75
  76.1 3.9 %pad_multiply_fusion.1 = f32[18,1,1,130,130]{4,3,2,1,0:T(8,128)S(1)} fusion(f32[18,1,1,128,128]{4,3,2,1,0:T(8,128)S(1)} %get-tuple-element.23, f32[20,1,3,128,128]{4,3,2,1,0:T(8,128)S(1)} %maximum_select_fusion), kind=kLoop, calls=%fused_computation.75 | loop fusion | flops 2129400 | bytes 6328608 | tf_op jit(solution)/shard_map/mul | solution.py:60
  80.0 3.1 %fusion.67 = (f32[16,1,1,128,128]{4,3,2,1,0:T(8,128)}, f32[16,1,1,128,128]{4,3,2,1,0:T(8,128)}, f32[16,1,1,128,128]{4,3,2,1,0:T(8,128)}) fusion(f32[18,1,1,130,130]{4,3,2,1,0:T(8,128)S(1)} %pad_multiply_fusion.1), kind=kLoop, calls=%fused_computation.153 | loop fusion | flops 1572864 | bytes 9437184 | tf_op jit(solution)/shard_map/mul | solution.py:63
  83.1 5.7 %fusion.9 = f32[16,1,3,128,128]{4,3,2,1,0:T(8,128)S(1)} fusion(f32[20,1,3,128,128]{4,3,2,1,0:T(8,128)S(1)} %maximum_select_fusion, f32[16,1,1,128,128]{4,3,2,1,0:T(8,128)} %get-tuple-element.34, f32[16,1,1,128,128]{4,3,2,1,0:T(8,128)} %get-tuple-element.35, f32[16,1,1,128,128]{4,3,2,1,0:T(8,128)} %get-tuple-element.33, ...), kind=kLoop, calls=%fused_computation.39 | loop fusion | flops 15728640 | bytes 25952256 | tf_op jit(solution)/shard_map/add | solution.py:64
  92.4 2.3 %copy.97 = f32[768,256]{1,0:T(8,128)} copy(f32[768,256]{0,1:T(8,128)} %bitcast.32) | data formatting | bytes 1572864 | tf_op jit(solution)/shard_map/dot_general | solution.py:87
  98.7 8.0 %concatenate.116 = f32[16,2,3,10,128]{4,3,2,1,0:T(8,128)} concatenate(f32[16,2,3,1,128]{4,3,2,1,0:T(1,128)} %broadcast_in_dim.74, f32[16,2,3,2,128]{4,3,2,1,0:T(2,128)} %get-tuple-element.67, f32[16,2,3,4,128]{4,3,2,1,0:T(4,128)} %concatenate.115, f32[16,2,3,2,128]{4,3,2,1,0:T(2,128)} %get-tuple-element.66, f32[16,2,3,1,128]{4,3,2,1,0:T(1,128)} %broadcast_in_dim.74), dimensions={3} | concatenate | bytes 983040 | tf_op jit(solution)/shard_map/concatenate | solution.py:90
  107.7 4.4 %collective-permute-start.9 = (f32[2,1,3,10,128]{4,3,2,1,0:T(8,128)S(1)}, f32[2,1,3,10,128]{4,3,2,1,0:T(8,128)S(1)}, u32[]{:S(2)}, u32[]{:S(2)}) collective-permute-start(f32[2,1,3,10,128]{4,3,2,1,0:T(8,128)S(1)} %get-tuple-element.41), channel_id=1, source_target_pairs={{1,0},{2,1},{3,2},{4,3},{5,4},{6,5},{7,6},{8,7},{9,8},{10,9},{11,1... | collective-permute-start | bytes 92168 | tf_op jit(solution)/shard_map/ppermute | solution.py:21
  112.1 4.4 %collective-permute-start.5 = (f32[2,1,3,10,128]{4,3,2,1,0:T(8,128)S(1)}, f32[2,1,3,10,128]{4,3,2,1,0:T(8,128)S(1)}, u32[]{:S(2)}, u32[]{:S(2)}) collective-permute-start(f32[2,1,3,10,128]{4,3,2,1,0:T(8,128)S(1)} %get-tuple-element.43), channel_id=1, source_target_pairs={{1,0},{2,1},{3,2},{4,3},{5,4},{6,5},{7,6},{8,7},{9,8},{10,9},{11,1... | collective-permute-start | bytes 92168 | tf_op jit(solution)/shard_map/ppermute | solution.py:21
  116.5 10.4 %collective-permute-start.4 = (f32[2,1,3,10,128]{4,3,2,1,0:T(8,128)S(1)}, f32[2,1,3,10,128]{4,3,2,1,0:T(8,128)S(1)}, u32[]{:S(2)}, u32[]{:S(2)}) collective-permute-start(f32[2,1,3,10,128]{4,3,2,1,0:T(8,128)S(1)} %get-tuple-element.40), channel_id=1, source_target_pairs={{0,1},{1,2},{2,3},{3,4},{4,5},{5,6},{6,7},{7,8},{8,9},{9,10},{10,1... | collective-permute-start | bytes 92168 | tf_op jit(solution)/shard_map/ppermute | solution.py:20
  128.2 5.0 %collective-permute-done.4 = f32[2,1,3,10,128]{4,3,2,1,0:T(8,128)S(1)} collective-permute-done((f32[2,1,3,10,128]{4,3,2,1,0:T(8,128)S(1)}, f32[2,1,3,10,128]{4,3,2,1,0:T(8,128)S(1)}, u32[]{:S(2)}, u32[]{:S(2)}) %collective-permute-start.4) | collective-permute-done | bytes 30752 | tf_op jit(solution)/shard_map/ppermute | solution.py:20
  141.3 3.7 %collective-permute-done.7 = f32[2,1,3,128,128]{4,3,2,1,0:T(8,128)S(1)} collective-permute-done((f32[2,1,3,128,128]{4,3,2,1,0:T(8,128)S(1)}, f32[2,1,3,128,128]{4,3,2,1,0:T(8,128)S(1)}, u32[]{:S(2)}, u32[]{:S(2)}) %collective-permute-start.7) | collective-permute-done | bytes 393248 | tf_op jit(solution)/shard_map/ppermute | solution.py:21
  145.0 4.7 %collective-permute-done.6 = f32[2,1,3,128,128]{4,3,2,1,0:T(8,128)S(1)} collective-permute-done((f32[2,1,3,128,128]{4,3,2,1,0:T(8,128)S(1)}, f32[2,1,3,128,128]{4,3,2,1,0:T(8,128)S(1)}, u32[]{:S(2)}, u32[]{:S(2)}) %collective-permute-start.6) | collective-permute-done | bytes 393248 | tf_op jit(solution)/shard_map/ppermute | solution.py:20
  150.4 3.9 %pad_multiply_fusion = f32[18,1,1,130,130]{4,3,2,1,0:T(8,128)S(1)} fusion(f32[18,1,1,128,128]{4,3,2,1,0:T(8,128)S(1)} %copy-done.4, f32[20,1,3,128,128]{4,3,2,1,0:T(8,128)S(1)} %maximum_select_fusion.1), kind=kLoop, calls=%fused_computation.74 | loop fusion | flops 2129400 | bytes 6328608 | tf_op jit(solution)/shard_map/mul | solution.py:60
  154.3 3.1 %fusion.64 = (f32[16,1,1,128,128]{4,3,2,1,0:T(8,128)}, f32[16,1,1,128,128]{4,3,2,1,0:T(8,128)}, f32[16,1,1,128,128]{4,3,2,1,0:T(8,128)}) fusion(f32[18,1,1,130,130]{4,3,2,1,0:T(8,128)S(1)} %pad_multiply_fusion), kind=kLoop, calls=%fused_computation.147 | loop fusion | flops 1572864 | bytes 9437184 | tf_op jit(solution)/shard_map/mul | solution.py:63
  157.4 6.1 %fusion.22 = f32[16,1,3,128,128]{4,3,2,1,0:T(8,128)S(1)} fusion(f32[20,1,3,128,128]{4,3,2,1,0:T(8,128)S(1)} %maximum_select_fusion.1, f32[16,1,1,128,128]{4,3,2,1,0:T(8,128)} %get-tuple-element.31, f32[16,1,1,128,128]{4,3,2,1,0:T(8,128)} %get-tuple-element.32, f32[16,1,1,128,128]{4,3,2,1,0:T(8,128)} %get-tuple-element.30, f32[16,128,128]{2,1,0:T(8,128)} %copy-done.11, ...), kind=kLoop, calls=%fused_computation.52 | loop fusion | flops 15728640 | bytes 25952256 | tf_op jit(solution)/shard_map/add | solution.py:64
  164.7 2.8 %fusion.37 = f32[16,1,3,128,128]{4,3,2,1,0:T(8,128)} fusion(f32[16,1,3,4,128]{4,3,2,1,0:T(4,128)S(1)} %get-tuple-element.12, f32[16,1,3,120,128]{4,3,2,1,0:T(8,128)S(1)} %slice.839, f32[16,1,3,4,128]{4,3,2,1,0:T(4,128)S(1)} %get-tuple-element.11, f32[16,1,3,128,128]{4,3,2,1,0:T(8,128)S(1)} %copy-done, f32[16,1,3,128,128]{4,3,2,1,0:T(8,128)S(1)} %fusion.36, ...), kind=kLoop, calls=%fused_computation.73 | loop fusion | flops 4718592 | bytes 13631488 | tf_op jit(solution)/shard_map/add | solution.py:199
  (115 shorter events, 34.4 us)
Async XLA Ops:
  0.0 35.6 %copy-start.17 = (s32[16,128,128]{2,1,0:T(8,128)S(1)}, s32[16,128,128]{2,1,0:T(8,128)}, u32[]{:S(2)}) copy-start(s32[16,128,128]{2,1,0:T(8,128)} %param.16) | copy-start | bytes 3145732
  4.4 23.5 %all-to-all-start = ((s32[16,16,1]{1,2,0:T(1,128)}), s32[16,16,1]{1,2,0:T(1,128)S(1)}, u32[]{:S(2)}, u32[]{:S(2)}) async-start(s32[16,16,1]{1,2,0:T(1,128)} %bitcast.26), calls=%async_computation | async-start | bytes 16384 | tf_op jit(solution)/shard_map/all_to_all | solution.py:81
  12.7 22.9 %collective-permute-start.1 = (s32[1,128,128]{2,1,0:T(8,128)S(1)}, s32[1,128,128]{2,1,0:T(8,128)S(1)}, u32[]{:S(2)}, u32[]{:S(2)}) collective-permute-start(s32[1,128,128]{2,1,0:T(8,128)S(1)} %get-tuple-element.39), channel_id=1, source_target_pairs={{1,0},{2,1},{3,2},{4,3},{5,4},{6,5},{7,6},{8,7},{9,8},{10,9},{11,1... | collective-permute-start | bytes 196616 | tf_op jit(solution)/shard_map/ppermute | solution.py:21
  17.1 18.5 %collective-permute-start = (s32[1,128,128]{2,1,0:T(8,128)S(1)}, s32[1,128,128]{2,1,0:T(8,128)S(1)}, u32[]{:S(2)}, u32[]{:S(2)}) collective-permute-start(s32[1,128,128]{2,1,0:T(8,128)S(1)} %get-tuple-element.38), channel_id=1, source_target_pairs={{0,1},{1,2},{2,3},{3,4},{4,5},{5,6},{6,7},{7,8},{8,9},{9,10},{10,1... | collective-permute-start | bytes 196616 | tf_op jit(solution)/shard_map/ppermute | solution.py:20
  19.2 54.6 %collective-permute-start.3 = (f32[2,1,3,128,128]{4,3,2,1,0:T(8,128)}, f32[2,1,3,128,128]{4,3,2,1,0:T(8,128)}, u32[]{:S(2)}, u32[]{:S(2)}) collective-permute-start(f32[2,1,3,128,128]{4,3,2,1,0:T(8,128)} %get-tuple-element.29), channel_id=1, source_target_pairs={{1,0},{2,1},{3,2},{4,3},{5,4},{6,5},{7,6},{8,7},{9,8},{10,9},{11,1... | collective-permute-start | bytes 1179656 | tf_op jit(solution)/shard_map/ppermute | solution.py:21
  23.6 50.1 %collective-permute-start.2 = (f32[2,1,3,128,128]{4,3,2,1,0:T(8,128)}, f32[2,1,3,128,128]{4,3,2,1,0:T(8,128)}, u32[]{:S(2)}, u32[]{:S(2)}) collective-permute-start(f32[2,1,3,128,128]{4,3,2,1,0:T(8,128)} %get-tuple-element.28), channel_id=1, source_target_pairs={{0,1},{1,2},{2,3},{3,4},{4,5},{5,6},{6,7},{7,8},{8,9},{9,10},{10,1... | collective-permute-start | bytes 1179656 | tf_op jit(solution)/shard_map/ppermute | solution.py:20
  27.9 64.5 %all-to-all-start.1 = ((f32[16,16,768]{2,1,0:T(8,128)}), f32[16,16,768]{2,1,0:T(8,128)}, u32[]{:S(2)}, u32[]{:S(2)}) async-start(f32[16,16,768]{2,1,0:T(8,128)} %bitcast.30), calls=%async_computation.1 | async-start | bytes 1572864 | tf_op jit(solution)/shard_map/all_to_all | solution.py:80
  41.2 10.7 %copy-start.23 = (f32[3,16]{1,0:T(4,128)S(1)}, f32[3,16]{1,0:T(4,128)}, u32[]{:S(2)}) copy-start(f32[3,16]{1,0:T(4,128)} %param.17) | copy-start | bytes 580
  70.0 6.1 %copy-start.3 = (f32[18,1,1,128,128]{4,3,2,1,0:T(8,128)}, f32[18,1,1,128,128]{4,3,2,1,0:T(8,128)S(1)}, u32[]{:S(2)}) copy-start(f32[18,1,1,128,128]{4,3,2,1,0:T(8,128)S(1)} %get-tuple-element.23) | copy-start | bytes 3538948
  73.7 9.4 %copy-start.5 = (f32[16,128,128]{2,1,0:T(8,128)}, f32[16,128,128]{2,1,0:T(8,128)S(1)}, u32[]{:S(2)}) copy-start(f32[16,128,128]{2,1,0:T(8,128)S(1)} %get-tuple-element.14) | copy-start | bytes 3145732
  73.7 9.4 %copy-start.7 = (f32[16,128,128]{2,1,0:T(8,128)}, f32[16,128,128]{2,1,0:T(8,128)S(1)}, u32[]{:S(2)}) copy-start(f32[16,128,128]{2,1,0:T(8,128)S(1)} %get-tuple-element.15) | copy-start | bytes 3145732
  73.7 9.4 %copy-start.9 = (f32[16,128,128]{2,1,0:T(8,128)}, f32[16,128,128]{2,1,0:T(8,128)S(1)}, u32[]{:S(2)}) copy-start(f32[16,128,128]{2,1,0:T(8,128)S(1)} %get-tuple-element.16) | copy-start | bytes 3145732
  73.7 9.4 %copy-start.11 = (f32[16,128,128]{2,1,0:T(8,128)}, f32[16,128,128]{2,1,0:T(8,128)S(1)}, u32[]{:S(2)}) copy-start(f32[16,128,128]{2,1,0:T(8,128)S(1)} %get-tuple-element.17) | copy-start | bytes 3145732
  73.7 9.4 %copy-start.12 = (f32[16,128,128]{2,1,0:T(8,128)}, f32[16,128,128]{2,1,0:T(8,128)S(1)}, u32[]{:S(2)}) copy-start(f32[16,128,128]{2,1,0:T(8,128)S(1)} %get-tuple-element.18) | copy-start | bytes 3145732
  73.7 9.4 %copy-start.13 = (f32[16,128,128]{2,1,0:T(8,128)}, f32[16,128,128]{2,1,0:T(8,128)S(1)}, u32[]{:S(2)}) copy-start(f32[16,128,128]{2,1,0:T(8,128)S(1)} %get-tuple-element.19) | copy-start | bytes 3145732
  106.8 26.7 %copy-start.21 = (f32[18,1,1,5,128]{4,3,2,1,0:T(8,128)S(1)}, f32[18,1,1,5,128]{4,3,2,1,0:T(8,128)}, u32[]{:S(2)}) copy-start(f32[18,1,1,5,128]{4,3,2,1,0:T(8,128)} %get-tuple-element.36) | copy-start | bytes 138244
  106.8 26.7 %copy-start.22 = (f32[18,1,1,5,128]{4,3,2,1,0:T(8,128)S(1)}, f32[18,1,1,5,128]{4,3,2,1,0:T(8,128)}, u32[]{:S(2)}) copy-start(f32[18,1,1,5,128]{4,3,2,1,0:T(8,128)} %get-tuple-element.37) | copy-start | bytes 138244
  107.7 20.5 %collective-permute-start.9 = (f32[2,1,3,10,128]{4,3,2,1,0:T(8,128)S(1)}, f32[2,1,3,10,128]{4,3,2,1,0:T(8,128)S(1)}, u32[]{:S(2)}, u32[]{:S(2)}) collective-permute-start(f32[2,1,3,10,128]{4,3,2,1,0:T(8,128)S(1)} %get-tuple-element.41), channel_id=1, source_target_pairs={{1,0},{2,1},{3,2},{4,3},{5,4},{6,5},{7,6},{8,7},{9,8},{10,9},{11,1... | collective-permute-start | bytes 92168 | tf_op jit(solution)/shard_map/ppermute | solution.py:21
  112.1 16.1 %collective-permute-start.8 = (f32[2,1,3,10,128]{4,3,2,1,0:T(8,128)S(1)}, f32[2,1,3,10,128]{4,3,2,1,0:T(8,128)S(1)}, u32[]{:S(2)}, u32[]{:S(2)}) collective-permute-start(f32[2,1,3,10,128]{4,3,2,1,0:T(8,128)S(1)} %get-tuple-element.42), channel_id=1, source_target_pairs={{0,1},{1,2},{2,3},{3,4},{4,5},{5,6},{6,7},{7,8},{8,9},{9,10},{10,1... | collective-permute-start | bytes 92168 | tf_op jit(solution)/shard_map/ppermute | solution.py:20
  112.1 16.1 %collective-permute-start.5 = (f32[2,1,3,10,128]{4,3,2,1,0:T(8,128)S(1)}, f32[2,1,3,10,128]{4,3,2,1,0:T(8,128)S(1)}, u32[]{:S(2)}, u32[]{:S(2)}) collective-permute-start(f32[2,1,3,10,128]{4,3,2,1,0:T(8,128)S(1)} %get-tuple-element.43), channel_id=1, source_target_pairs={{1,0},{2,1},{3,2},{4,3},{5,4},{6,5},{7,6},{8,7},{9,8},{10,9},{11,1... | collective-permute-start | bytes 92168 | tf_op jit(solution)/shard_map/ppermute | solution.py:21
  116.5 16.6 %collective-permute-start.4 = (f32[2,1,3,10,128]{4,3,2,1,0:T(8,128)S(1)}, f32[2,1,3,10,128]{4,3,2,1,0:T(8,128)S(1)}, u32[]{:S(2)}, u32[]{:S(2)}) collective-permute-start(f32[2,1,3,10,128]{4,3,2,1,0:T(8,128)S(1)} %get-tuple-element.40), channel_id=1, source_target_pairs={{0,1},{1,2},{2,3},{3,4},{4,5},{5,6},{6,7},{7,8},{8,9},{9,10},{10,1... | collective-permute-start | bytes 92168 | tf_op jit(solution)/shard_map/ppermute | solution.py:20
  139.6 5.4 %collective-permute-start.7 = (f32[2,1,3,128,128]{4,3,2,1,0:T(8,128)S(1)}, f32[2,1,3,128,128]{4,3,2,1,0:T(8,128)S(1)}, u32[]{:S(2)}, u32[]{:S(2)}) collective-permute-start(f32[2,1,3,128,128]{4,3,2,1,0:T(8,128)S(1)} %get-tuple-element.27), channel_id=1, source_target_pairs={{1,0},{2,1},{3,2},{4,3},{5,4},{6,5},{7,6},{8,7},{9,8},{10,9},{11,1... | collective-permute-start | bytes 1179656 | tf_op jit(solution)/shard_map/ppermute | solution.py:21
  139.7 10.0 %collective-permute-start.6 = (f32[2,1,3,128,128]{4,3,2,1,0:T(8,128)S(1)}, f32[2,1,3,128,128]{4,3,2,1,0:T(8,128)S(1)}, u32[]{:S(2)}, u32[]{:S(2)}) collective-permute-start(f32[2,1,3,128,128]{4,3,2,1,0:T(8,128)S(1)} %get-tuple-element.26), channel_id=1, source_target_pairs={{0,1},{1,2},{2,3},{3,4},{4,5},{5,6},{6,7},{7,8},{8,9},{9,10},{10,1... | collective-permute-start | bytes 1179656 | tf_op jit(solution)/shard_map/ppermute | solution.py:20
  141.3 9.0 %copy-start.4 = (f32[18,1,1,128,128]{4,3,2,1,0:T(8,128)S(1)}, f32[18,1,1,128,128]{4,3,2,1,0:T(8,128)}, u32[]{:S(2)}) copy-start(f32[18,1,1,128,128]{4,3,2,1,0:T(8,128)} %copy-done.3) | copy-start | bytes 3538948
  (12 other events, 29.3 us)
where the time goes:
time: 170 us; the launch traced here: 168 us
  other arithmetic  53.4 us (31%)
  starting transfers between devices  41.9 us (25%)
  local copies, waits for them, and re-layouts  38.4 us (23%)
  matrix products  19.2 us (11%)
  waiting for transfers between devices  13.3 us (8%)
    ppermute x5, starting transfers between devices, padded(): after = lax.ppermute(leading, axis, down)  17.8 us
    dot_general x1, matrix products, material(): jnp.dot(table, onehot, precision=HIGHEST, preferred_element_type=jnp.floa...  17.3 us
    unnamed x50, local copies, waits for them, and re-layouts  14.5 us
    add x2, other arithmetic, elastic(): return diffusion + jnp.concatenate(pushes, axis=2)  11.8 us
    ppermute x5, starting transfers between devices, padded(): before = lax.ppermute(last, axis, up)  10.9 us
    ppermute x5, waiting for transfers between devices, padded(): before = lax.ppermute(last, axis, up)  9.66 us
    mul x3, other arithmetic, elastic(): flux = bulk * spread  9.6 us
    concatenate x2, local copies, waits for them, and re-layouts, receive(): jnp.concatenate([blank, summed[:, :, :, 0:2], blank, blank, blank, blank,...  8.73 us
  transfers between devices with their start and end apart: 12, of which 3 were waited for; matrix products, arithmetic and copies ran while one was open for 39% of the time, Pallas kernels for 0%

commit v1 on v0

v1 whole, which is shorter than its diff:
```python
import functools

import jax
import jax.numpy as jnp
from jax import lax
from jax.experimental import pallas as pl
from jax.experimental.pallas import tpu as pltpu
from jax.sharding import PartitionSpec as P

SPAN = 4
TIME_STEP = 0.04
HIGHEST = lax.Precision.HIGHEST
MESH = pl.DeviceIdType.MESH


def above(a, axis):
    size = a.shape[axis]
    at = lax.broadcasted_iota(jnp.int32, a.shape, axis)
    return jnp.where(at == size - 1, 0.0, pltpu.roll(a, size - 1, axis))


def below(a, axis, edge=0.0):
    at = lax.broadcasted_iota(jnp.int32, a.shape, axis)
    return jnp.where(at == 0, edge, pltpu.roll(a, 1, axis))


def volume(xp, xm, vy, vz, bulk):
    total = (xp - xm) + (above(vy, 0) - below(vy, 0)) + (above(vz, 1) - below(vz, 1))
    return bulk * total


def elastic(now, nxt, prv, half, half_nxt, half_prv, g, g_nxt, g_prv):
    face_xp = half + half_nxt
    face_xm = half + half_prv
    face_y = half + above(half, 0)
    face_z = half + above(half, 1)
    push = (
        g_nxt - g_prv,
        above(g, 0) - below(g, 0),
        above(g, 1) - below(g, 1),
    )
    result = []
    for i in range(3):
        v = now[i]
        total = face_xp * (nxt[i] - v) - face_xm * (v - prv[i])
        edge = half * v
        for axis, face in ((0, face_y), (1, face_z)):
            flow = face * (above(v, axis) - v)
            total = total + (flow - below(flow, axis, edge))
        result.append(total + push[i])
    return result


def body(
    count,
    cap,
    regional_ref,
    weight_ref,
    seg_ref,
    col_ref,
    owner_ref,
    table_ref,
    class_ref,
    prev_ref,
    now_ref,
    out_ref,
    cls,
    before,
    d0,
    d1,
    half,
    bulk,
    inv,
    g,
    mat,
    band0,
    band1,
    delta,
    gs,
    send,
    recv,
    local_sem,
    a2a_send,
    a2a_recv,
    halo_send,
    halo_recv,
):
    me = lax.axis_index("tile")
    position = lax.rem(me + count - SPAN // 2, SPAN)
    right = lax.rem(me + 1, count)
    left = lax.rem(me + count - 1, count)
    planes, depth = cls.shape[0], cls.shape[2]
    across = cls.shape[1]
    has_left, has_right = position > 0, position < SPAN - 1

    load_now = pltpu.make_async_copy(now_ref, d0.at[pl.ds(2, planes)], local_sem.at[0])
    load_class = pltpu.make_async_copy(class_ref, cls, local_sem.at[1])
    load_prev = pltpu.make_async_copy(prev_ref, before, local_sem.at[2])
    load_now.start()
    load_class.start()
    load_prev.start()

    barrier = pltpu.get_barrier_semaphore()

    def greet(k, carry):
        pl.semaphore_signal(
            barrier, inc=1, device_id={"tile": lax.rem(me + k, count)}, device_id_type=MESH
        )
        return carry

    lax.fori_loop(1, count, greet, 0)

    rows = regional_ref.shape[0]
    boxes = owner_ref.shape[1]
    seg = seg_ref[...]
    box_ids = lax.broadcasted_iota(jnp.int32, (rows, boxes), 1)
    owner = jnp.sum(
        jnp.where(seg // SPAN == box_ids, owner_ref[...], 0), axis=1, keepdims=True
    )
    target = lax.rem(owner * SPAN + SPAN // 2 + lax.rem(seg, SPAN), count)
    tile_ids = lax.broadcasted_iota(jnp.int32, (rows, count), 1)
    chosen = jnp.where(target == tile_ids, 1.0, 0.0)
    lower = jnp.where(
        lax.broadcasted_iota(jnp.int32, (rows, rows), 0)
        > lax.broadcasted_iota(jnp.int32, (rows, rows), 1),
        1.0,
        0.0,
    )
    earlier = jnp.dot(lower, chosen, preferred_element_type=jnp.float32)
    rank = jnp.sum(earlier * chosen, axis=1, keepdims=True)
    slots = count * cap
    slot = target.astype(jnp.float32) * cap + rank
    slot_ids = lax.broadcasted_iota(jnp.int32, (rows, slots), 1).astype(jnp.float32)
    place = jnp.where(slot == slot_ids, 1.0, 0.0)
    weighted = regional_ref[...] * weight_ref[...]
    over_rows = (((0,), (0,)), ((), ()))
    outgoing = lax.dot_general(
        place, weighted, over_rows, precision=HIGHEST, preferred_element_type=jnp.float32
    )
    chunks = weighted.shape[1] // depth
    for k in range(chunks):
        send[:, k * cap : (k + 1) * cap, :] = outgoing[:, k * depth : (k + 1) * depth].reshape(
            count, cap, depth
        )
    lane = lax.broadcasted_iota(jnp.int32, (rows, depth), 1)
    lane = (lane - lax.rem(me * cap, depth)).astype(jnp.float32)
    marks = jnp.where(lane == rank, (col_ref[...] + 1).astype(jnp.float32), 0.0)
    columns = lax.dot_general(
        chosen, marks, over_rows, precision=HIGHEST, preferred_element_type=jnp.float32
    )
    send[:, chunks * cap : chunks * cap + 8, :] = jnp.broadcast_to(
        columns[:, None, :], (count, 8, depth)
    )

    pl.semaphore_wait(barrier, count - 1)

    def block_copy(k):
        return pltpu.make_async_remote_copy(
            src_ref=send.at[lax.rem(me + k, count)],
            dst_ref=recv.at[me],
            send_sem=a2a_send.at[k],
            recv_sem=a2a_recv.at[k],
            device_id={"tile": lax.rem(me + k, count)},
            device_id_type=MESH,
        )

    def halo(ref, width, which):
        extent = ref.shape[0]
        to_right = pltpu.make_async_remote_copy(
            src_ref=ref.at[pl.ds(extent - 2 * width, width)],
            dst_ref=ref.at[pl.ds(0, width)],
            send_sem=halo_send.at[2 * which],
            recv_sem=halo_recv.at[2 * which],
            device_id={"tile": right},
            device_id_type=MESH,
        )
        to_left = pltpu.make_async_remote_copy(
            src_ref=ref.at[pl.ds(width, width)],
            dst_ref=ref.at[pl.ds(extent - width, width)],
            send_sem=halo_send.at[2 * which + 1],
            recv_sem=halo_recv.at[2 * which + 1],
            device_id={"tile": left},
            device_id_type=MESH,
        )
        return to_right, to_left

    halos = {
        "now": halo(d0, 2, 0),
        "half": halo(half, 1, 1),
        "bulk": halo(bulk, 1, 2),
        "mat": halo(mat, 3, 3),
        "next": halo(d1, 2, 4),
        "band0": halo(band0, 4, 5),
        "band1": halo(band1, 2, 6),
    }

    def start(*names):
        @pl.when(has_right)
        def _():
            for name in names:
                halos[name][0].start()

        @pl.when(has_left)
        def _():
            for name in names:
                halos[name][1].start()

    def arrive(*names):
        @pl.when(has_left)
        def _():
            for name in names:
                halos[name][0].wait_recv()

        @pl.when(has_right)
        def _():
            for name in names:
                halos[name][1].wait_recv()

    def sent(*names):
        @pl.when(has_right)
        def _():
            for name in names:
                halos[name][0].wait_send()

        @pl.when(has_left)
        def _():
            for name in names:
                halos[name][1].wait_send()

    rims = ((d0, 2), (half, 1), (bulk, 1), (mat, 3), (d1, 2), (band0, 4), (band1, 2))

    @pl.when(jnp.logical_not(has_left))
    def _():
        for ref, width in rims:
            ref[0:width] = jnp.zeros((width,) + ref.shape[1:], jnp.float32)

    @pl.when(jnp.logical_not(has_right))
    def _():
        for ref, width in rims:
            extent = ref.shape[0]
            ref[extent - width : extent] = jnp.zeros((width,) + ref.shape[1:], jnp.float32)

    load_now.wait()
    start("now")

    def launch(k, carry):
        block_copy(k).start()
        return carry

    lax.fori_loop(1, count, launch, 0)
    recv[me] = send[me]
    load_class.wait()

    tables = [
        jnp.broadcast_to(table_ref[k : k + 1, :], (across, table_ref.shape[1])) for k in range(3)
    ]

    def look_up(p, carry):
        ids = cls[p]
        lam, mu, irho = [jnp.take_along_axis(t, ids, axis=1) for t in tables]
        values = (0.5 * mu, 0.25 * (lam + mu), TIME_STEP * irho)
        half[p + 1], bulk[p + 1], inv[p] = values
        for k in range(3):
            mat[p + 3, k, 0:8] = values[k][0:8]
            mat[p + 3, k, 8:16] = values[k][across - 8 : across]
        return carry

    lax.fori_loop(0, planes, look_up, 0)
    start("half", "bulk", "mat")

    def strain(d, p):
        g[p] = volume(d[p + 2, 0], d[p, 0], d[p + 1, 1], d[p + 1, 2], bulk[p])

    def advance(d, p):
        now = [d[p + 2, i] for i in range(3)]
        nxt = [d[p + 3, i] for i in range(3)]
        prv = [d[p + 1, i] for i in range(3)]
        return now, elastic(
            now, nxt, prv, half[p + 1], half[p + 2], half[p], g[p + 1], g[p + 2], g[p]
        )

    def first(p):
        now, forces = advance(d0, p)
        for i in range(3):
            d1[p + 2, i] = 2.0 * now[i] - before[p, i] + inv[p] * forces[i]

    def second(p):
        now, forces = advance(d1, p)
        for i in range(3):
            out_ref[p, i] = 2.0 * now[i] - d0[p + 2, i] + inv[p] * forces[i]

    def sweep(d, update, middle):
        if middle:
            lax.fori_loop(2, planes, lambda p, c: (strain(d, p), c)[1], 0)
            lax.fori_loop(2, planes - 2, lambda p, c: (update(p), c)[1], 0)
        else:
            jump = planes - 2

            lax.fori_loop(
                0, 4, lambda k, c: (strain(d, k + (k // 2) * jump), c)[1], 0
            )
            lax.fori_loop(
                0, 4, lambda k, c: (update(k + (k // 2) * (planes - 4)), c)[1], 0
            )

    load_prev.wait()
    sweep(d0, first, True)
    arrive("now", "half", "bulk")
    sweep(d0, first, False)
    start("next")
    sweep(d1, second, True)

    def land(k, carry):
        block_copy(k).wait_recv()
        return carry

    lax.fori_loop(1, count, land, 0)
    marked = recv[:, chunks * cap : chunks * cap + 8, :]
    row_in = lax.broadcasted_iota(jnp.int32, marked.shape, 1)
    marked = jnp.where(row_in == 0, marked, 0.0)
    group = depth // cap
    parts = [
        jnp.sum(marked[k : k + group].reshape(-1, depth), axis=0, keepdims=True)
        for k in range(0, count, group)
    ]
    sources = jnp.concatenate(parts, axis=1)
    ids = lax.broadcasted_iota(jnp.int32, (planes * 16, 1), 0)
    at, x4 = lax.rem(ids, 16), (ids // 16) * 4 + 1
    wanted = jnp.where(
        at == 1,
        x4,
        jnp.where(at == 2, x4 + 1, jnp.where(at == 13, x4 + 2, jnp.where(at == 14, x4 + 3, -1))),
    ).astype(jnp.float32)
    picks = jnp.where(wanted == sources, 1.0, 0.0)
    for k in range(chunks):
        rows_k = recv[:, k * cap : (k + 1) * cap, :].reshape(slots, depth)
        field = jnp.dot(picks, rows_k, precision=HIGHEST, preferred_element_type=jnp.float32)
        field = field.reshape(planes, 16, depth)
        if k < 3:
            band0[4 : 4 + planes, k] = field
        else:
            band1[2 : 2 + planes, k - 3] = field
    start("band0", "band1")

    arrive("next")
    sweep(d1, second, False)
    arrive("mat", "band0", "band1")

    slab_row = lax.broadcasted_iota(jnp.int32, (16, depth), 0)
    outer = jnp.where(jnp.logical_or(slab_row < 2, slab_row >= 14), 1.0, 0.0)
    inner = 1.0 - outer

    def force(ref, x, m):
        total = None
        for take, keep in ((outer, inner), (inner, -outer)):
            field = [[ref[x + dx, i] * take for i in range(3)] for dx in (-1, 0, 1)]
            far = [ref[x + dx, 0] * take for dx in (-2, 2)]
            g_prv = volume(field[1][0], far[0], field[0][1], field[0][2], mat[m - 1, 1])
            g_now = volume(field[2][0], field[0][0], field[1][1], field[1][2], mat[m, 1])
            g_nxt = volume(far[1], field[1][0], field[2][1], field[2][2], mat[m + 1, 1])
            parts = elastic(
                field[1], field[2], field[0], mat[m, 0], mat[m + 1, 0], mat[m - 1, 0],
                g_now, g_nxt, g_prv,
            )
            parts = [keep * part for part in parts]
            total = parts if total is None else [a + b for a, b in zip(total, parts)]
        return total

    def first_change(q, carry):
        push = force(band0, q + 2, q + 1)
        for i in range(3):
            delta[q, i] = mat[q + 1, 2] * push[i]
        return carry

    lax.fori_loop(0, planes + 4, first_change, 0)

    def slab_strain(q, carry):
        gs[q] = volume(
            delta[q + 2, 0], delta[q, 0], delta[q + 1, 1], delta[q + 1, 2], mat[q + 2, 1]
        )
        return carry

    lax.fori_loop(0, planes + 2, slab_strain, 0)

    def second_change(p, carry):
        push = force(band1, p + 2, p + 3)
        now = [delta[p + 2, i] for i in range(3)]
        nxt = [delta[p + 3, i] for i in range(3)]
        prv = [delta[p + 1, i] for i in range(3)]
        spread = elastic(
            now, nxt, prv, mat[p + 3, 0], mat[p + 4, 0], mat[p + 2, 0],
            gs[p + 1], gs[p + 2], gs[p],
        )
        for i in range(3):
            change = 2.0 * now[i] + mat[p + 3, 2] * (spread[i] + push[i])
            out_ref[p, i, 0:8] += change[0:8]
            out_ref[p, i, across - 8 : across] += change[8:16]
        return carry

    lax.fori_loop(0, planes, second_change, 0)

    sent("now", "half", "bulk", "mat", "next", "band0", "band1")

    def leave(k, carry):
        block_copy(k).wait_send()
        return carry

    lax.fori_loop(1, count, leave, 0)


def shards(
    regional,
    row_weight,
    row_seg,
    row_col,
    box_owner,
    cell_class,
    soil_props,
    build_props,
    real_ids,
    disp_prev,
    disp_now,
):
    count = lax.axis_size("tile")
    planes, _, _, across, depth = disp_now.shape
    capacity = max(2, 2 * regional.shape[0] // count)
    cap = -(-capacity // 8) * 8
    block = 6 * cap + 8
    table = jnp.concatenate([soil_props, build_props[real_ids[0]]], axis=1)
    table = jnp.pad(table, ((0, 5), (0, depth - table.shape[1])))
    plane = (across, depth)
    f32 = jnp.float32
    vmem = pl.BlockSpec(memory_space=pltpu.VMEM)
    hbm = pl.BlockSpec(memory_space=pl.ANY)
    result = pl.pallas_call(
        functools.partial(body, count, cap),
        out_shape=jax.ShapeDtypeStruct((planes, 3) + plane, f32),
        in_specs=[vmem] * 6 + [hbm] * 3,
        out_specs=vmem,
        scratch_shapes=[
            pltpu.VMEM((planes,) + plane, jnp.int32),
            pltpu.VMEM((planes, 3) + plane, f32),
            pltpu.VMEM((planes + 4, 3) + plane, f32),
            pltpu.VMEM((planes + 4, 3) + plane, f32),
            pltpu.VMEM((planes + 2,) + plane, f32),
            pltpu.VMEM((planes + 2,) + plane, f32),
            pltpu.VMEM((planes,) + plane, f32),
            pltpu.VMEM((planes + 2,) + plane, f32),
            pltpu.VMEM((planes + 6, 3, 16, depth), f32),
            pltpu.VMEM((planes + 8, 3, 16, depth), f32),
            pltpu.VMEM((planes + 4, 3, 16, depth), f32),
            pltpu.VMEM((planes + 4, 3, 16, depth), f32),
            pltpu.VMEM((planes + 2, 16, depth), f32),
            pltpu.VMEM((count, block, depth), f32),
            pltpu.VMEM((count, block, depth), f32),
            pltpu.SemaphoreType.DMA((3,)),
            pltpu.SemaphoreType.DMA((count,)),
            pltpu.SemaphoreType.DMA((count,)),
            pltpu.SemaphoreType.DMA((14,)),
            pltpu.SemaphoreType.DMA((14,)),
        ],
        compiler_params=pltpu.CompilerParams(
            collective_id=0, has_side_effects=True, vmem_limit_bytes=56 * 1024 * 1024
        ),
        cost_estimate=pl.CostEstimate(
            flops=200 * planes * across * depth * 3,
            bytes_accessed=40 * planes * across * depth,
            transcendentals=0,
        ),
    )(
        regional,
        row_weight,
        row_seg,
        row_col,
        box_owner[None],
        table,
        cell_class,
        disp_prev.reshape((planes, 3) + plane),
        disp_now.reshape((planes, 3) + plane),
    )
    return result.reshape(disp_now.shape)


def solution(mesh):
    row = P(("scen", "tile"), None)
    cell = P(("scen", "tile"), None, None)
    field = P(("scen", "tile"), None, None, None, None)
    return jax.shard_map(
        shards,
        mesh=mesh,
        in_specs=(row, row, row, row, P("scen"), cell, P(), P(), P("scen"), field, field),
        out_specs=field,
        check_vma=False,
    )
```

time: 170 us -> 64.3 us (0.38); the launches traced: 168 us -> 63.9 us
  Pallas kernels: 0 us -> 53.7 us
  other arithmetic: 53.4 us -> 1.33 us
  starting transfers between devices: 41.9 us -> 0 us
  local copies, waits for them, and re-layouts: 38.4 us -> 8.17 us
  matrix products: 19.2 us -> 0 us
  waiting for transfers between devices: 13.3 us -> 0 us
    pallas_call x0 -> x1, Pallas kernels: none -> 53.7 us  [shards(): pl.pallas_call(functools.partial(body, count, cap), out_shape=jax.ShapeDt...]
    ppermute x10 -> x0, starting transfers between devices: 28.7 us -> none  [the longest x5 17.8 us: padded(): after = lax.ppermute(leading, axis, down)]
    mul x11 -> x0, other arithmetic: 19.6 us -> none  [the longest x3 9.6 us: elastic(): flux = bulk * spread]
    dot_general x3 -> x0, matrix products: 19.2 us -> none  [the longest x1 17.3 us: material(): jnp.dot(table, onehot, precision=HIGHEST, preferred_element_type=jnp.floa...]
    add x6 -> x0, other arithmetic: 17.3 us -> none  [the longest x2 11.8 us: elastic(): return diffusion + jnp.concatenate(pushes, axis=2)]
    ppermute x10 -> x0, waiting for transfers between devices: 13.3 us -> none  [the longest x5 9.66 us: padded(): before = lax.ppermute(last, axis, up)]
    all_to_all x2 -> x0, starting transfers between devices: 13.2 us -> none  [the longest x1 7.39 us: receive(): lax.all_to_all(columns, 'tile', split_axis=0, concat_axis=0, tiled=True)]
    slice x10 -> x0, local copies, waits for them, and re-layouts: 8.91 us -> none  [the longest x4 3.9 us: padded(): last = lax.slice_in_dim(value, length - width, length, axis=dim)]
  transfers between devices with their start and end apart: 12 -> 0, of which waited for: 3 -> 0; matrix products, arithmetic and copies ran while one was open for 39% -> 0% of each run, Pallas kernels for 0% -> 0%
where the time goes in v1:
time: 64.3 us; the launch traced here: 63.9 us
  Pallas kernels  53.7 us (84%)
  local copies, waits for them, and re-layouts  8.17 us (13%)
  other arithmetic  1.33 us (2%)
  between operations  0.68 us (1%)
    pallas_call x1, Pallas kernels, shards(): pl.pallas_call(functools.partial(body, count, cap), out_shape=jax.ShapeDt...  53.7 us
    unnamed x7, local copies, waits for them, and re-layouts  8.17 us
    concatenate x1, other arithmetic, shards(): table = jnp.concatenate([soil_props, build_props[real_ids[0]]], axis=1)  1.33 us

profile of v1, /device:TPU:0, one launch (start us, length us, event | category | flops | bytes accessed | tf_op | source)
XLA Modules:
  0.0 63.9 jit_solution(18364161989157859210)
XLA Ops:
  0.0 0.0 copy-start
  0.7 0.1 copy-done
  0.8 1.3 %select_maximum_fusion.table_ref = f32[8,128]{1,0:T(8,128)} fusion(f32[3,16]{1,0:T(4,128)S(1)} %bitcast.16, f32[3,16]{1,0:T(4,128)} %param.17), kind=kLoop, calls=%fused_computation | loop fusion | flops 8192 | bytes 4480 | tf_op jit(solution)/shard_map/concatenate | solution.py:429
  2.1 1.4 %copy.16.weight_ref = f32[128,1]{1,0:T(8,128)} copy(f32[128,1]{0,1:T(1,128)} %param.12) | data formatting | bytes 1024 | tf_op args[1]
  3.5 1.4 %copy.17.seg_ref = s32[128,1]{1,0:T(8,128)} copy(s32[128,1]{0,1:T(1,128)} %param.13) | data formatting | bytes 1024 | tf_op args[2]
  4.9 1.4 %copy.18.col_ref = s32[128,1]{1,0:T(8,128)} copy(s32[128,1]{0,1:T(1,128)} %param.14) | data formatting | bytes 1024 | tf_op args[3]
  6.3 53.7 %shard_map.109 = f32[16,3,128,128]{3,2,1,0:T(8,128)} custom-call(f32[128,768]{1,0:T(8,128)} %regional_ref.1, f32[128,1]{1,0:T(8,128)} %copy.16.weight_ref, s32[128,1]{1,0:T(8,128)} %copy.17.seg_ref, s32[128,1]{1,0:T(8,128)} %copy.18.col_ref, s32[1,4]{1,0:T(1,128)} %bitcast.17, f32[8,128]{1,0:T(8,128)} %select_maximum_fusion.table_ref, ...), custom_call_target="tpu_custom_call" | custom-call | flops 157286400 | bytes 10485760 | tf_op jit(solution)/shard_map/pallas_call | solution.py:435
  60.0 3.9 %copy.25 = f32[16,1,3,128,128]{4,3,2,1,0:T(8,128)} copy(f32[16,1,3,128,128]{4,3,2,1,0:T(8,128)} %bitcast.13) | data formatting | bytes 6291456
  (2 shorter events, 0.0 us)
Async XLA Ops:
  0.0 0.8 %copy-start = (f32[16,3,16]{2,0,1:T(8,128)S(1)}, f32[16,3,16]{2,0,1:T(8,128)}, u32[]{:S(2)}) copy-start(f32[16,3,16]{2,0,1:T(8,128)} %param.18) | copy-start | bytes 9220

commit v2 on v1

--- a/solution.py
+++ b/solution.py
@@ -59,12 +59,15 @@
     seg_ref,
     col_ref,
     owner_ref,
-    table_ref,
+    soil_ref,
+    build_ref,
+    real_ref,
     class_ref,
     prev_ref,
     now_ref,
     out_ref,
     cls,
+    slab_cls,
     before,
     d0,
     d1,
@@ -75,6 +78,8 @@
     mat,
     band0,
     band1,
+    edge_out,
+    edge_in,
     delta,
     gs,
     send,
@@ -89,15 +94,24 @@
     position = lax.rem(me + count - SPAN // 2, SPAN)
     right = lax.rem(me + 1, count)
     left = lax.rem(me + count - 1, count)
-    planes, depth = cls.shape[0], cls.shape[2]
-    across = cls.shape[1]
+    planes, across, depth = inv.shape
     has_left, has_right = position > 0, position < SPAN - 1
 
     load_now = pltpu.make_async_copy(now_ref, d0.at[pl.ds(2, planes)], local_sem.at[0])
-    load_class = pltpu.make_async_copy(class_ref, cls, local_sem.at[1])
+    load_class = pltpu.make_async_copy(class_ref, cls.at[pl.ds(1, planes)], local_sem.at[1])
+    load_low = pltpu.make_async_copy(
+        class_ref.at[:, pl.ds(0, 8)], slab_cls.at[pl.ds(3, planes), pl.ds(0, 8)], local_sem.at[3]
+    )
+    load_high = pltpu.make_async_copy(
+        class_ref.at[:, pl.ds(across - 8, 8)],
+        slab_cls.at[pl.ds(3, planes), pl.ds(8, 8)],
+        local_sem.at[4],
+    )
     load_prev = pltpu.make_async_copy(prev_ref, before, local_sem.at[2])
+    load_low.start()
+    load_high.start()
+    load_class.start()
     load_now.start()
-    load_class.start()
     load_prev.start()
 
     barrier = pltpu.get_barrier_semaphore()
@@ -113,40 +127,41 @@
     rows = regional_ref.shape[0]
     boxes = owner_ref.shape[1]
     seg = seg_ref[...]
-    box_ids = lax.broadcasted_iota(jnp.int32, (rows, boxes), 1)
-    owner = jnp.sum(
-        jnp.where(seg // SPAN == box_ids, owner_ref[...], 0), axis=1, keepdims=True
-    )
+    owner = jnp.zeros_like(seg)
+    for box in range(boxes):
+        owner = jnp.where(seg // SPAN == box, owner_ref[0, box], owner)
     target = lax.rem(owner * SPAN + SPAN // 2 + lax.rem(seg, SPAN), count)
-    tile_ids = lax.broadcasted_iota(jnp.int32, (rows, count), 1)
+    tile_ids = lax.broadcasted_iota(jnp.int32, (count, rows), 0)
     chosen = jnp.where(target == tile_ids, 1.0, 0.0)
-    lower = jnp.where(
+    upper = jnp.where(
         lax.broadcasted_iota(jnp.int32, (rows, rows), 0)
-        > lax.broadcasted_iota(jnp.int32, (rows, rows), 1),
+        < lax.broadcasted_iota(jnp.int32, (rows, rows), 1),
         1.0,
         0.0,
     )
-    earlier = jnp.dot(lower, chosen, preferred_element_type=jnp.float32)
-    rank = jnp.sum(earlier * chosen, axis=1, keepdims=True)
+    earlier = jnp.dot(chosen, upper, preferred_element_type=jnp.float32)
+    rank = jnp.sum(earlier * chosen, axis=0, keepdims=True)
     slots = count * cap
     slot = target.astype(jnp.float32) * cap + rank
-    slot_ids = lax.broadcasted_iota(jnp.int32, (rows, slots), 1).astype(jnp.float32)
-    place = jnp.where(slot == slot_ids, 1.0, 0.0)
-    weighted = regional_ref[...] * weight_ref[...]
-    over_rows = (((0,), (0,)), ((), ()))
-    outgoing = lax.dot_general(
-        place, weighted, over_rows, precision=HIGHEST, preferred_element_type=jnp.float32
-    )
-    chunks = weighted.shape[1] // depth
+    slot_ids = lax.broadcasted_iota(jnp.int32, (slots, rows), 0).astype(jnp.float32)
+    place = jnp.where(slot == slot_ids, weight_ref[...], 0.0)
+    outgoing = jnp.dot(
+        place, regional_ref[...], precision=HIGHEST, preferred_element_type=jnp.float32
+    )
+    chunks = regional_ref.shape[1] // depth
     for k in range(chunks):
         send[:, k * cap : (k + 1) * cap, :] = outgoing[:, k * depth : (k + 1) * depth].reshape(
             count, cap, depth
         )
-    lane = lax.broadcasted_iota(jnp.int32, (rows, depth), 1)
+    lane = lax.broadcasted_iota(jnp.int32, (depth, rows), 0)
     lane = (lane - lax.rem(me * cap, depth)).astype(jnp.float32)
-    marks = jnp.where(lane == rank, (col_ref[...] + 1).astype(jnp.float32), 0.0)
+    marks = jnp.where(lane == rank, 1.0, 0.0)
     columns = lax.dot_general(
-        chosen, marks, over_rows, precision=HIGHEST, preferred_element_type=jnp.float32
+        chosen * (col_ref[...] + 1).astype(jnp.float32),
+        marks,
+        (((1,), (1,)), ((), ())),
+        precision=HIGHEST,
+        preferred_element_type=jnp.float32,
     )
     send[:, chunks * cap : chunks * cap + 8, :] = jnp.broadcast_to(
         columns[:, None, :], (count, 8, depth)
@@ -164,19 +179,18 @@
             device_id_type=MESH,
         )
 
-    def halo(ref, width, which):
-        extent = ref.shape[0]
+    def pair(which, from_low, to_high, from_high, to_low):
         to_right = pltpu.make_async_remote_copy(
-            src_ref=ref.at[pl.ds(extent - 2 * width, width)],
-            dst_ref=ref.at[pl.ds(0, width)],
+            src_ref=from_high,
+            dst_ref=to_low,
             send_sem=halo_send.at[2 * which],
             recv_sem=halo_recv.at[2 * which],
             device_id={"tile": right},
             device_id_type=MESH,
         )
         to_left = pltpu.make_async_remote_copy(
-            src_ref=ref.at[pl.ds(width, width)],
-            dst_ref=ref.at[pl.ds(extent - width, width)],
+            src_ref=from_low,
+            dst_ref=to_high,
             send_sem=halo_send.at[2 * which + 1],
             recv_sem=halo_recv.at[2 * which + 1],
             device_id={"tile": left},
@@ -184,14 +198,25 @@
         )
         return to_right, to_left
 
+    def halo(ref, width, which):
+        extent = ref.shape[0]
+        spans = [width, extent - width, extent - 2 * width, 0]
+        return pair(which, *[ref.at[pl.ds(at, width)] for at in spans])
+
+    def near(d, which):
+        return pair(which, d.at[2], d.at[planes + 2], d.at[planes + 1], d.at[1])
+
+    def far(d, which):
+        return pair(which, d.at[3, 0], d.at[planes + 3, 0], d.at[planes, 0], d.at[0, 0])
+
     halos = {
-        "now": halo(d0, 2, 0),
-        "half": halo(half, 1, 1),
-        "bulk": halo(bulk, 1, 2),
-        "mat": halo(mat, 3, 3),
-        "next": halo(d1, 2, 4),
-        "band0": halo(band0, 4, 5),
-        "band1": halo(band1, 2, 6),
+        "class": halo(cls, 1, 0),
+        "slab": halo(slab_cls, 3, 1),
+        "near0": near(d0, 2),
+        "far0": far(d0, 3),
+        "near1": near(d1, 4),
+        "far1": far(d1, 5),
+        "edge": pair(6, edge_out.at[0], edge_in.at[1], edge_out.at[1], edge_in.at[0]),
     }
 
     def start(*names):
@@ -227,7 +252,7 @@
             for name in names:
                 halos[name][1].wait_send()
 
-    rims = ((d0, 2), (half, 1), (bulk, 1), (mat, 3), (d1, 2), (band0, 4), (band1, 2))
+    rims = ((d0, 2), (half, 1), (bulk, 1), (mat, 3), (d1, 2), (edge_in, 1))
 
     @pl.when(jnp.logical_not(has_left))
     def _():
@@ -240,8 +265,11 @@
             extent = ref.shape[0]
             ref[extent - width : extent] = jnp.zeros((width,) + ref.shape[1:], jnp.float32)
 
+    load_low.wait()
+    load_high.wait()
+    load_class.wait()
     load_now.wait()
-    start("now")
+    start("class", "slab", "near0", "far0")
 
     def launch(k, carry):
         block_copy(k).start()
@@ -249,24 +277,35 @@
 
     lax.fori_loop(1, count, launch, 0)
     recv[me] = send[me]
-    load_class.wait()
-
-    tables = [
-        jnp.broadcast_to(table_ref[k : k + 1, :], (across, table_ref.shape[1])) for k in range(3)
-    ]
+
+    entry = lax.broadcasted_iota(jnp.int32, build_ref.shape[1:], 0) == real_ref[0]
+    tables = []
+    for k in range(3):
+        chosen_build = jnp.sum(jnp.where(entry, build_ref[k], 0.0), axis=0, keepdims=True)
+        both = jnp.concatenate([soil_ref[k : k + 1, :], chosen_build], axis=1)
+        blank = jnp.zeros((1, depth - both.shape[1]), jnp.float32)
+        both = jnp.concatenate([both, blank], axis=1)
+        tables.append(jnp.broadcast_to(both, (across, depth)))
+
+    def properties(ids):
+        lam, mu, irho = [
+            jnp.take_along_axis(t[0 : ids.shape[0]], ids, axis=1) for t in tables
+        ]
+        return 0.5 * mu, 0.25 * (lam + mu), TIME_STEP * irho
 
     def look_up(p, carry):
-        ids = cls[p]
-        lam, mu, irho = [jnp.take_along_axis(t, ids, axis=1) for t in tables]
-        values = (0.5 * mu, 0.25 * (lam + mu), TIME_STEP * irho)
-        half[p + 1], bulk[p + 1], inv[p] = values
-        for k in range(3):
-            mat[p + 3, k, 0:8] = values[k][0:8]
-            mat[p + 3, k, 8:16] = values[k][across - 8 : across]
+        half[p + 1], bulk[p + 1], inv[p] = properties(cls[p + 1])
+        return carry
+
+    def look_up_rim(e):
+        half[e], bulk[e], _ = properties(cls[e])
+
+    def look_up_slab(e, carry):
+        mat[e, 0], mat[e, 1], mat[e, 2] = properties(slab_cls[e])
         return carry
 
     lax.fori_loop(0, planes, look_up, 0)
-    start("half", "bulk", "mat")
+    lax.fori_loop(3, planes + 3, look_up_slab, 0)
 
     def strain(d, p):
         g[p] = volume(d[p + 2, 0], d[p, 0], d[p + 1, 1], d[p + 1, 2], bulk[p])
@@ -305,9 +344,20 @@
 
     load_prev.wait()
     sweep(d0, first, True)
-    arrive("now", "half", "bulk")
+    arrive("class", "slab", "near0", "far0")
+
+    @pl.when(has_left)
+    def _():
+        look_up_rim(0)
+        lax.fori_loop(0, 3, look_up_slab, 0)
+
+    @pl.when(has_right)
+    def _():
+        look_up_rim(planes + 1)
+        lax.fori_loop(planes + 3, planes + 6, look_up_slab, 0)
+
     sweep(d0, first, False)
-    start("next")
+    start("near1", "far1")
     sweep(d1, second, True)
 
     def land(k, carry):
@@ -331,20 +381,41 @@
         x4,
         jnp.where(at == 2, x4 + 1, jnp.where(at == 13, x4 + 2, jnp.where(at == 14, x4 + 3, -1))),
     ).astype(jnp.float32)
-    picks = jnp.where(wanted == sources, 1.0, 0.0)
+    rim = lax.broadcasted_iota(jnp.int32, (32, 1), 0)
+    rim = (rim + (rim // 16) * (4 * planes - 32) + 1).astype(jnp.float32)
+    picks = jnp.where(jnp.concatenate([wanted, rim], axis=0) == sources, 1.0, 0.0)
     for k in range(chunks):
         rows_k = recv[:, k * cap : (k + 1) * cap, :].reshape(slots, depth)
         field = jnp.dot(picks, rows_k, precision=HIGHEST, preferred_element_type=jnp.float32)
-        field = field.reshape(planes, 16, depth)
+        edge_out[0, k] = field[planes * 16 : planes * 16 + 16]
+        edge_out[1, k] = field[planes * 16 + 16 : planes * 16 + 32]
+        field = field[0 : planes * 16].reshape(planes, 16, depth)
         if k < 3:
             band0[4 : 4 + planes, k] = field
         else:
             band1[2 : 2 + planes, k - 3] = field
-    start("band0", "band1")
-
-    arrive("next")
+    start("edge")
+
+    arrive("near1", "far1")
     sweep(d1, second, False)
-    arrive("mat", "band0", "band1")
+    arrive("edge")
+    spread = jnp.where(
+        wanted[0:64]
+        == (lax.broadcasted_iota(jnp.int32, (1, 16), 1) + 1).astype(jnp.float32),
+        1.0,
+        0.0,
+    )
+    for side in range(2):
+        for k in range(chunks):
+            field = jnp.dot(
+                spread, edge_in[side, k], precision=HIGHEST, preferred_element_type=jnp.float32
+            ).reshape(4, 16, depth)
+            if k < 3:
+                at_plane = side * (planes + 4)
+                band0[at_plane : at_plane + 4, k] = field
+            else:
+                at_plane = side * (planes + 2)
+                band1[at_plane : at_plane + 2, k - 3] = field[0:2] if side else field[2:4]
 
     slab_row = lax.broadcasted_iota(jnp.int32, (16, depth), 0)
     outer = jnp.where(jnp.logical_or(slab_row < 2, slab_row >= 14), 1.0, 0.0)
@@ -399,7 +470,7 @@
 
     lax.fori_loop(0, planes, second_change, 0)
 
-    sent("now", "half", "bulk", "mat", "next", "band0", "band1")
+    sent("class", "slab", "near0", "far0", "near1", "far1", "edge")
 
     def leave(k, carry):
         block_copy(k).wait_send()
@@ -426,19 +497,19 @@
     capacity = max(2, 2 * regional.shape[0] // count)
     cap = -(-capacity // 8) * 8
     block = 6 * cap + 8
-    table = jnp.concatenate([soil_props, build_props[real_ids[0]]], axis=1)
-    table = jnp.pad(table, ((0, 5), (0, depth - table.shape[1])))
     plane = (across, depth)
     f32 = jnp.float32
     vmem = pl.BlockSpec(memory_space=pltpu.VMEM)
+    smem = pl.BlockSpec(memory_space=pltpu.SMEM)
     hbm = pl.BlockSpec(memory_space=pl.ANY)
     result = pl.pallas_call(
         functools.partial(body, count, cap),
         out_shape=jax.ShapeDtypeStruct((planes, 3) + plane, f32),
-        in_specs=[vmem] * 6 + [hbm] * 3,
+        in_specs=[vmem] * 4 + [smem] + [vmem] * 2 + [smem] + [hbm] * 3,
         out_specs=vmem,
         scratch_shapes=[
-            pltpu.VMEM((planes,) + plane, jnp.int32),
+            pltpu.VMEM((planes + 2,) + plane, jnp.int32),
+            pltpu.VMEM((planes + 6, 16, depth), jnp.int32),
             pltpu.VMEM((planes, 3) + plane, f32),
             pltpu.VMEM((planes + 4, 3) + plane, f32),
             pltpu.VMEM((planes + 4, 3) + plane, f32),
@@ -449,11 +520,13 @@
             pltpu.VMEM((planes + 6, 3, 16, depth), f32),
             pltpu.VMEM((planes + 8, 3, 16, depth), f32),
             pltpu.VMEM((planes + 4, 3, 16, depth), f32),
+            pltpu.VMEM((2, 6, 16, depth), f32),
+            pltpu.VMEM((2, 6, 16, depth), f32),
             pltpu.VMEM((planes + 4, 3, 16, depth), f32),
             pltpu.VMEM((planes + 2, 16, depth), f32),
             pltpu.VMEM((count, block, depth), f32),
             pltpu.VMEM((count, block, depth), f32),
-            pltpu.SemaphoreType.DMA((3,)),
+            pltpu.SemaphoreType.DMA((5,)),
             pltpu.SemaphoreType.DMA((count,)),
             pltpu.SemaphoreType.DMA((count,)),
             pltpu.SemaphoreType.DMA((14,)),
@@ -469,11 +542,13 @@
         ),
     )(
         regional,
-        row_weight,
-        row_seg,
-        row_col,
+        row_weight.reshape(1, -1),
+        row_seg.reshape(1, -1),
+        row_col.reshape(1, -1),
         box_owner[None],
-        table,
+        soil_props,
+        jnp.transpose(build_props, (1, 0, 2)),
+        real_ids,
         cell_class,
         disp_prev.reshape((planes, 3) + plane),
         disp_now.reshape((planes, 3) + plane),

time: 64.3 us -> 56 us (0.87)
  local copies, waits for them, and re-layouts: 8.17 us -> 3.91 us
  Pallas kernels: 53.7 us -> 51.2 us
  other arithmetic: 1.33 us -> 0 us
    unnamed x7 -> x1, local copies, waits for them, and re-layouts: 8.17 us -> 3.91 us
    pallas_call x1, Pallas kernels: 53.7 us -> 51.2 us  [shards(): pl.pallas_call(functools.partial(body, count, cap), out_shape=jax.ShapeDt...]
    concatenate x1 -> x0, other arithmetic: 1.33 us -> none  [shards(): table = jnp.concatenate([soil_props, build_props[real_ids[0]]], axis=1)]
where the time goes in v2:
time: 56 us; the launch traced here: 55.8 us
  Pallas kernels  51.2 us (91%)
  local copies, waits for them, and re-layouts  3.91 us (7%)
  between operations  0.66 us (1%)
    pallas_call x1, Pallas kernels, shards(): pl.pallas_call(functools.partial(body, count, cap), out_shape=jax.ShapeDt...  51.2 us
    unnamed x1, local copies, waits for them, and re-layouts  3.91 us

profile of v2, /device:TPU:0, one launch (start us, length us, event | category | flops | bytes accessed | tf_op | source)
XLA Modules:
  0.0 55.8 jit_solution(11279154886828262870)
XLA Ops:
  0.7 51.2 %shard_map.109 = f32[16,3,128,128]{3,2,1,0:T(8,128)} custom-call(f32[128,768]{1,0:T(8,128)} %regional_ref.1, f32[1,128]{1,0:T(1,128)} %bitcast.14, s32[1,128]{1,0:T(1,128)} %bitcast.15, s32[1,128]{1,0:T(1,128)} %bitcast.16, s32[1,4]{1,0:T(1,128)} %bitcast.17, f32[3,16]{1,0:T(4,128)} %soil_ref.1, f32[3,16,16]{2,1,0:T(8,128)} %bitcast.13, ...), custom_call_target="tpu_custom_call" | custom-call | flops 157286400 | bytes 10485760 | tf_op jit(solution)/shard_map/pallas_call | solution.py:505
  51.9 3.9 %copy.15 = f32[16,1,3,128,128]{4,3,2,1,0:T(8,128)} copy(f32[16,1,3,128,128]{4,3,2,1,0:T(8,128)} %bitcast.10) | data formatting | bytes 6291456

commit v3 on v2

--- a/solution.py
+++ b/solution.py
@@ -377,9 +377,9 @@
     ids = lax.broadcasted_iota(jnp.int32, (planes * 16, 1), 0)
     at, x4 = lax.rem(ids, 16), (ids // 16) * 4 + 1
     wanted = jnp.where(
-        at == 1,
+        at == 2,
         x4,
-        jnp.where(at == 2, x4 + 1, jnp.where(at == 13, x4 + 2, jnp.where(at == 14, x4 + 3, -1))),
+        jnp.where(at == 1, x4 + 1, jnp.where(at == 14, x4 + 2, jnp.where(at == 13, x4 + 3, -1))),
     ).astype(jnp.float32)
     rim = lax.broadcasted_iota(jnp.int32, (32, 1), 0)
     rim = (rim + (rim // 16) * (4 * planes - 32) + 1).astype(jnp.float32)
@@ -418,24 +418,32 @@
                 band1[at_plane : at_plane + 2, k - 3] = field[0:2] if side else field[2:4]
 
     slab_row = lax.broadcasted_iota(jnp.int32, (16, depth), 0)
-    outer = jnp.where(jnp.logical_or(slab_row < 2, slab_row >= 14), 1.0, 0.0)
-    inner = 1.0 - outer
+    outside = jnp.logical_or(slab_row < 2, slab_row >= 14)
+    sign = jnp.where(outside, -1.0, 1.0)
+    downward = lax.rem(slab_row, 12) == 1
+    turn = jnp.where(downward, 1.0, -1.0)
+
+    def across_to(a):
+        return jnp.where(downward, pltpu.roll(a, 15, 0), pltpu.roll(a, 1, 0))
 
     def force(ref, x, m):
-        total = None
-        for take, keep in ((outer, inner), (inner, -outer)):
-            field = [[ref[x + dx, i] * take for i in range(3)] for dx in (-1, 0, 1)]
-            far = [ref[x + dx, 0] * take for dx in (-2, 2)]
-            g_prv = volume(field[1][0], far[0], field[0][1], field[0][2], mat[m - 1, 1])
-            g_now = volume(field[2][0], field[0][0], field[1][1], field[1][2], mat[m, 1])
-            g_nxt = volume(far[1], field[1][0], field[2][1], field[2][2], mat[m + 1, 1])
-            parts = elastic(
-                field[1], field[2], field[0], mat[m, 0], mat[m + 1, 0], mat[m - 1, 0],
-                g_now, g_nxt, g_prv,
-            )
-            parts = [keep * part for part in parts]
-            total = parts if total is None else [a + b for a, b in zip(total, parts)]
-        return total
+        fields = [[sign * ref[x + dx, i] for i in range(3)] for dx in (-1, 0, 1)]
+        prv, now, nxt = fields
+        g_prv, g_now, g_nxt = [
+            turn * mat[m + dx, 1] * fields[dx + 1][1] for dx in (-1, 0, 1)
+        ]
+        face = mat[m, 0] + across_to(mat[m, 0])
+        source = (nxt[0] - prv[0]) + (above(now[2], 1) - below(now[2], 1))
+        source = turn * across_to(mat[m, 1]) * source
+        reach = mat[m, 1] * now[1]
+        reach = pltpu.roll(jnp.where(downward, reach, 0.0), 15, 0) + pltpu.roll(
+            jnp.where(downward, 0.0, reach), 1, 0
+        )
+        return (
+            face * now[0] + (g_nxt - g_prv),
+            face * now[1] + source + reach,
+            face * now[2] + (above(g_now, 1) - below(g_now, 1)),
+        )
 
     def first_change(q, carry):
         push = force(band0, q + 2, q + 1)

time: 56 us -> 53.5 us (0.955)
  Pallas kernels: 51.2 us -> 48.7 us
    pallas_call x1, Pallas kernels: 51.2 us -> 48.7 us  [shards(): pl.pallas_call(functools.partial(body, count, cap), out_shape=jax.ShapeDt...]
where the time goes in v3:
time: 53.5 us; the launch traced here: 53.3 us
  Pallas kernels  48.7 us (91%)
  local copies, waits for them, and re-layouts  3.91 us (7%)
  between operations  0.66 us (1%)
    pallas_call x1, Pallas kernels, shards(): pl.pallas_call(functools.partial(body, count, cap), out_shape=jax.ShapeDt...  48.7 us
    unnamed x1, local copies, waits for them, and re-layouts  3.91 us

profile of v3, /device:TPU:0, one launch (start us, length us, event | category | flops | bytes accessed | tf_op | source)
XLA Modules:
  0.0 53.3 jit_solution(16539795063181358463)
XLA Ops:
  0.7 48.7 %shard_map.109 = f32[16,3,128,128]{3,2,1,0:T(8,128)} custom-call(f32[128,768]{1,0:T(8,128)} %regional_ref.1, f32[1,128]{1,0:T(1,128)} %bitcast.14, s32[1,128]{1,0:T(1,128)} %bitcast.15, s32[1,128]{1,0:T(1,128)} %bitcast.16, s32[1,4]{1,0:T(1,128)} %bitcast.17, f32[3,16]{1,0:T(4,128)} %soil_ref.1, f32[3,16,16]{2,1,0:T(8,128)} %bitcast.13, ...), custom_call_target="tpu_custom_call" | custom-call | flops 157286400 | bytes 10485760 | tf_op jit(solution)/shard_map/pallas_call | solution.py:513
  49.4 3.9 %copy.15 = f32[16,1,3,128,128]{4,3,2,1,0:T(8,128)} copy(f32[16,1,3,128,128]{4,3,2,1,0:T(8,128)} %bitcast.10) | data formatting | bytes 6291456
